TPU v7x, 32 devices: a whole 2x2x4 slice. The times are simulated.
32 devices in a mesh: gx: 4 (over y, x), gy: 8 (over z, core).
Axes of the slice: x: 2, y: 2, z: 4, core: 2. Of those that a mesh axis runs over, the one named last changes fastest.
Arguments:
- e_field: float32 [3, 32, 256, 512], P(None, 'gx', 'gy'), may hold values from -6 to 6
- h_field: float32 [3, 32, 256, 512], P(None, 'gx', 'gy'), may hold values from -6 to 6
- polar: float32 [3, 32, 256, 512], P(None, 'gx', 'gy'), may hold values from -6 to 6
- polar_prev: float32 [3, 32, 256, 512], P(None, 'gx', 'gy'), may hold values from -6 to 6
- material: int32 [32, 256, 512], P('gx', 'gy'), may hold values from 0 to 3
- eps_table: float32 [4], replicated, may hold values from 1 to 6
- delta_table: float32 [4], replicated, may hold values from 0.5 to 4
- omega_table: float32 [4], replicated, may hold values from 0.2 to 1.2
- damping_table: float32 [4], replicated, may hold values from 0.02 to 0.6
- surface_flags: int32 [4, 8], P('gx', 'gy'), may hold values 0 or 1
Outputs:
- e_out: float32 [3, 32, 256, 512], P(None, 'gx', 'gy')
- h_out: float32 [3, 32, 256, 512], P(None, 'gx', 'gy')
- polar_out: float32 [3, 32, 256, 512], P(None, 'gx', 'gy')
- far_field: float32 [2, 2, 4, 16384], replicated
All inputs are finite; a program needn't handle non-finite values. No bound on the sum of `surface_flags` on one device may be relied on, other than what follows from the above.
Results may differ from a plain program's by a relative error of at most 0.0003.
Values sent between devices are 32-bit elements; how exact they have to be, the bound alone decides.
A program may use at most 256 MiB of HBM per device.

v0:
```python
import math

import jax
import jax.numpy as jnp
from jax import lax
from jax.sharding import PartitionSpec as P

NTH = 64
NPH = 256
NDIR = 16384
ZS = 384


DT = 0.55
WAVELENGTHS = (5.0, 4.0)


def shifted(shard, axis, by):
    peers = lax.axis_size(axis)
    pairs = [(i, i + by) for i in range(peers) if 0 <= i + by < peers]
    return lax.ppermute(shard, axis, pairs)


def ahead(field, plane, axis):
    rest = lax.slice_in_dim(field, 1, field.shape[axis], axis=axis)
    return jnp.concatenate([rest, plane], axis=axis) - field


def behind(field, plane, axis):
    rest = lax.slice_in_dim(field, 0, field.shape[axis] - 1, axis=axis)
    return field - jnp.concatenate([plane, rest], axis=axis)


def zero_plane(field, axis):
    shape = list(field.shape)
    shape[axis] = 1
    return jnp.zeros(shape, jnp.float32)


def coefficients(eps_table, delta_table, omega_table, damping_table):
    half = damping_table * (DT / 2.0)
    denom = 1.0 + half
    square = omega_table * omega_table * (DT * DT)
    return (
        (2.0 - square) / denom,
        (half - 1.0) / denom,
        delta_table * square / denom,
        1.0 / eps_table,
    )


def curl_e(ex, ey, ez, xnext, ynext):
    zplane = zero_plane(ex, 2)
    curl_x = ahead(ez, ynext[1], 1) - ahead(ey, zplane, 2)
    curl_y = ahead(ex, zplane, 2) - ahead(ez, xnext[1], 0)
    curl_z = ahead(ey, xnext[0], 0) - ahead(ex, ynext[0], 1)
    return (curl_x, curl_y, curl_z)


def curl_h(hx, hy, hz, xprev, yprev):
    zplane = zero_plane(hx, 2)
    curl_x = behind(hz, yprev[1], 1) - behind(hy, zplane, 2)
    curl_y = behind(hx, zplane, 2) - behind(hz, xprev[1], 0)
    curl_z = behind(hy, xprev[0], 0) - behind(hx, yprev[0], 1)
    return (curl_x, curl_y, curl_z)


def directions(start, count):
    index = start + jnp.arange(count, dtype=jnp.int32)
    theta = ((index // NPH).astype(jnp.float32) + 0.5) * (math.pi / 2.0 / NTH)
    phi = ((index % NPH).astype(jnp.float32) + 0.5) * (2.0 * math.pi / NPH)
    return (jnp.sin(theta) * jnp.cos(phi), jnp.sin(theta) * jnp.sin(phi))


def lookup(material, table, count):
    result = jnp.zeros(material.shape, jnp.float32)
    for index in range(count):
        result = result + jnp.where(material == index, table[index], 0.0)
    return result


def next_planes(ex, ey, ez):
    xface = shifted(jnp.stack([ey[:1], ez[:1]]), "gx", -1)
    yface = shifted(jnp.stack([ex[:, :1], ez[:, :1]]), "gy", -1)
    return ((xface[0], xface[1]), (yface[0], yface[1]))


def prev_planes(hx, hy, hz):
    xface = shifted(jnp.stack([hy[-1:], hz[-1:]]), "gx", 1)
    yface = shifted(jnp.stack([hx[:, -1:], hz[:, -1:]]), "gy", 1)
    return ((xface[0], xface[1]), (yface[0], yface[1]))


def project_cells(real_acc, imag_acc, xvalues, yvalues, start, count):
    rows_x = xvalues.shape[0]
    rows_y = yvalues.shape[0]
    cells = rows_x * rows_y
    real_flat = real_acc.reshape(2, 4, cells)
    imag_flat = imag_acc.reshape(2, 4, cells)
    width = math.gcd(count, 2048)
    blocks = count // width

    def project(offset):
        dir_x, dir_y = directions(start + offset, width)
        parts = []
        for f in range(2):
            wave = 2.0 * math.pi / WAVELENGTHS[f]
            along_x = wave * xvalues[:, None] * dir_x[None, :]
            along_y = wave * yvalues[:, None] * dir_y[None, :]
            cos_x = jnp.cos(along_x)
            sin_x = jnp.sin(along_x)
            cos_y = jnp.cos(along_y)
            sin_y = jnp.sin(along_y)
            cosine = (
                cos_x[:, None, :] * cos_y[None, :, :] - sin_x[:, None, :] * sin_y[None, :, :]
            ).reshape(cells, width)
            sine = (
                sin_x[:, None, :] * cos_y[None, :, :] + cos_x[:, None, :] * sin_y[None, :, :]
            ).reshape(cells, width)
            hi = lax.Precision.HIGHEST
            real_part = jnp.dot(real_flat[f], cosine, precision=hi) - jnp.dot(
                imag_flat[f], sine, precision=hi
            )
            imag_part = jnp.dot(real_flat[f], sine, precision=hi) + jnp.dot(
                imag_flat[f], cosine, precision=hi
            )
            parts.append(jnp.stack([real_part, imag_part]))
        return jnp.stack(parts)

    offsets = jnp.arange(blocks, dtype=jnp.int32) * width
    pieces = lax.map(project, offsets)
    return jnp.moveaxis(pieces, 0, 3).reshape(2, 2, 4, count)


def shards(
    e_field,
    h_field,
    polar,
    polar_prev,
    material,
    eps_table,
    delta_table,
    omega_table,
    damping_table,
    surface_flags,
):
    cells_x = e_field.shape[1]
    cells_y = e_field.shape[2]
    count = eps_table.shape[0]
    coef_a, coef_b, coef_c, coef_inv = coefficients(
        eps_table, delta_table, omega_table, damping_table
    )
    vox_a = lookup(material, coef_a, count)
    vox_b = lookup(material, coef_b, count)
    vox_c = lookup(material, coef_c, count)
    vox_inv = lookup(material, coef_inv, count)
    flag = surface_flags[0, 0].astype(jnp.float32)
    ex, ey, ez = (e_field[0], e_field[1], e_field[2])
    hx, hy, hz = (h_field[0], h_field[1], h_field[2])
    pols = [polar[0], polar[1], polar[2]]
    prevs = [polar_prev[0], polar_prev[1], polar_prev[2]]
    real_acc = jnp.zeros((2, 4, cells_x, cells_y), jnp.float32)
    imag_acc = jnp.zeros((2, 4, cells_x, cells_y), jnp.float32)
    for step in range(2):
        xnext, ynext = next_planes(ex, ey, ez)
        curl_x, curl_y, curl_z = curl_e(ex, ey, ez, xnext, ynext)
        hx = hx - DT * curl_x
        hy = hy - DT * curl_y
        hz = hz - DT * curl_z
        fields = [ex, ey, ez]
        newpol = [vox_a * pols[i] + vox_b * prevs[i] + vox_c * fields[i] for i in range(3)]
        xprev, yprev = prev_planes(hx, hy, hz)
        curls = curl_h(hx, hy, hz, xprev, yprev)
        fields = [fields[i] + (DT * curls[i] - (newpol[i] - pols[i])) * vox_inv for i in range(3)]
        ex, ey, ez = fields
        prevs = pols
        pols = newpol
        surface = jnp.stack([-hy[:, :, ZS], hx[:, :, ZS], ey[:, :, ZS], -ex[:, :, ZS]]) * flag
        moment = (step + 1) * DT
        real_acc = real_acc + jnp.stack(
            [surface * math.cos(2.0 * math.pi / WAVELENGTHS[f] * moment) for f in range(2)]
        )
        imag_acc = imag_acc - jnp.stack(
            [surface * math.sin(2.0 * math.pi / WAVELENGTHS[f] * moment) for f in range(2)]
        )
    xglobal = (lax.axis_index("gx") * cells_x + jnp.arange(cells_x, dtype=jnp.int32)).astype(
        jnp.float32
    )
    yglobal = (lax.axis_index("gy") * cells_y + jnp.arange(cells_y, dtype=jnp.int32)).astype(
        jnp.float32
    )
    partial_far = project_cells(real_acc, imag_acc, xglobal, yglobal, 0, NDIR)
    total = lax.psum(partial_far, ("gx", "gy"))
    grid_x = cells_x * lax.axis_size("gx")
    grid_y = cells_y * lax.axis_size("gy")
    far_field = total * (1.0 / math.sqrt(grid_x * grid_y))
    return (jnp.stack([ex, ey, ez]), jnp.stack([hx, hy, hz]), jnp.stack(pols), far_field)


def solution(mesh):
    placed = (
        P(None, "gx", "gy", None),
        P(None, "gx", "gy", None),
        P(None, "gx", "gy", None),
        P(None, "gx", "gy", None),
        P("gx", "gy", None),
        P(),
        P(),
        P(),
        P(),
        P("gx", "gy"),
    )
    return jax.shard_map(
        shards,
        mesh=mesh,
        in_specs=placed,
        out_specs=(
            P(None, "gx", "gy", None),
            P(None, "gx", "gy", None),
            P(None, "gx", "gy", None),
            P(),
        ),
        check_vma=False,
    )
```

profile of v0, /device:TPU:0, one launch (start us, length us, event | category | flops | bytes accessed | tf_op | source)
XLA Modules:
  0.0 399.2 jit_solution(10119303926188444393)
XLA Ops:
  7.3 1.6 slice_bitcast_fusion.1
  9.0 1.3 collective-permute-start.1
  10.3 1.3 collective-permute-start
  19.7 3.1 fusion.46
  23.1 3.0 collective-permute-start.2
  28.5 6.1 %collective-permute-start.3 = (f32[2,1,32,512]{3,2,1,0:T(8,128)}, f32[2,1,32,512]{3,2,1,0:T(8,128)}, u32[]{:S(2)}, u32[]{:S(2)}) collective-permute-start(f32[2,1,32,512]{3,2,1,0:T(8,128)} %pad_maximum_fusion.3), channel_id=1, source_target_pairs={{0,8},{8,16},{16,24},{1,9},{9,17},{17,25},{2,10},{10,18},{18,26},{... | collective-permute-start | bytes 393224 | tf_op jit(solution)/shard_map/ppermute | solution.py:21
  35.9 13.2 %fusion.51 = (f32[8,32,512]{2,1,0:T(8,128)S(1)}, f32[8,32,512]{2,1,0:T(8,128)}, pred[8,32,512]{2,1,0:T(8,128)(4,1)S(1)}, pred[8,32,512]{2,1,0:T(8,128)(4,1)S(1)}...) fusion(f32[8,32,512]{2,1,0:T(8,128)S(1)} %get-tuple-element.169, f32[8,31,512]{2,1,0:T(8,128)S(1)} %bitcast.335, ...), kind=kLoop, calls=%fused_computation.90 | loop fusion | flops 6029312 | bytes 5766208 | tf_op jit(solution)/shard_map/add | solution.py:174
  51.7 1.3 stack.241
  54.8 13.0 %fusion.64 = (f32[8,32,512]{2,1,0:T(8,128)S(1)}, f32[8,32,512]{2,1,0:T(8,128)}) fusion(f32[8,32,512]{2,1,0:T(8,128)S(1)} %get-tuple-element.170, f32[7,32,512]{2,1,0:T(8,128)} %slice.432, f32[1,32,512]{2,1,0:T(8,128)S(1)} %get-tuple-element.184, f32[8,32,512]{2,1,0:T(8,128)S(1)} %get-tuple-element.168, f32[8,31,512]{2,1,0:T(8,128)S(1)} %bitcast.328, ...), kind=kLoop, calls=%fused_computation.106 | loop fusion | flops 5636096 | bytes 5242944 | tf_op jit(solution)/shard_map/add | solution.py:174
  68.7 12.8 %fusion.59 = (f32[8,32,512]{2,1,0:T(8,128)S(1)}, f32[8,32,512]{2,1,0:T(8,128)}) fusion(f32[8,32,512]{2,1,0:T(8,128)S(1)} %get-tuple-element.169, f32[7,32,512]{2,1,0:T(8,128)S(1)} %copy-done.22, f32[1,32,512]{2,1,0:T(8,128)S(1)} %get-tuple-element.183, f32[8,32,512]{2,1,0:T(8,128)S(1)} %get-tuple-element.168, f32[8,32,511]{2,1,0:T(8,128)S(1)} %bitcast.329, ...), kind=kLoop, calls=%fused_computation.100 | loop fusion | flops 5505024 | bytes 5241920 | tf_op jit(solution)/shard_map/add | solution.py:174
  82.5 1.4 collective-permute-start.5
  85.6 1.3 slice.441
  86.8 1.2 slice.443
  88.2 1.3 collective-permute-start.4
  89.5 5.8 %collective-permute-done.4 = f32[2,1,32,512]{3,2,1,0:T(8,128)S(1)} collective-permute-done((f32[2,1,32,512]{3,2,1,0:T(8,128)S(1)}, f32[2,1,32,512]{3,2,1,0:T(8,128)S(1)}, u32[]{:S(2)}, u32[]{:S(2)}) %collective-permute-start.4) | collective-permute-done | bytes 131104 | tf_op jit(solution)/shard_map/ppermute | solution.py:21
  96.5 2.9 collective-permute-start.6
  99.4 1.3 pad_maximum_fusion.1
  102.3 4.8 %collective-permute-start.7 = (f32[2,1,32,512]{3,2,1,0:T(8,128)S(1)}, f32[2,1,32,512]{3,2,1,0:T(8,128)S(1)}, u32[]{:S(2)}, u32[]{:S(2)}) collective-permute-start(f32[2,1,32,512]{3,2,1,0:T(8,128)S(1)} %pad_maximum_fusion.5), channel_id=1, source_target_pairs={{0,8},{8,16},{16,24},{1,9},{9,17},{17,25},{2,10},{10,18},{18,26},{... | collective-permute-start | bytes 393224 | tf_op jit(solution)/shard_map/ppermute | solution.py:21
  107.3 12.9 %fusion.75 = (f32[8,32,512]{2,1,0:T(8,128)S(1)}, f32[8,32,512]{2,1,0:T(8,128)}) fusion(f32[8,32,512]{2,1,0:T(8,128)S(1)} %copy-done.3, f32[8,32,512]{2,1,0:T(8,128)S(1)} %get-tuple-element.177, f32[8,31,512]{2,1,0:T(8,128)S(1)} %bitcast.334, f32[8,1,512]{2,1,0:T(1,128)S(1)} %get-tuple-element.187, f32[8,32,512]{2,1,0:T(8,128)} %get-tuple-element.137, ...), kind=kLoop, calls=%fused_computation.122 | loop fusion | flops 5505024 | bytes 5241920 | tf_op jit(solution)/shard_map/add | solution.py:174
  121.3 12.9 %fusion.83 = (f32[8,32,512]{2,1,0:T(8,128)S(1)}, f32[8,32,512]{2,1,0:T(8,128)}) fusion(f32[8,32,512]{2,1,0:T(8,128)S(1)} %copy-done.7, f32[8,32,512]{2,1,0:T(8,128)S(1)} %get-tuple-element.177, f32[7,32,512]{2,1,0:T(8,128)} %slice.456, f32[1,32,512]{2,1,0:T(8,128)S(1)} %get-tuple-element.179, f32[8,32,512]{2,1,0:T(8,128)} %get-tuple-element.143, ...), kind=kLoop, calls=%fused_computation.132 | loop fusion | flops 5505024 | bytes 5241920 | tf_op jit(solution)/shard_map/add | solution.py:174
  135.0 122.4 %while.13 = (s32[]{:T(128)}, f32[8,2,2,4,2048]{4,3,2,1,0:T(4,128)}, s32[8]{0:T(128)S(1)}, f32[2,4,256]{2,1,0:T(4,128)S(1)}, f32[2,4,256]{2,1,0:T(4,128)S(1)}, /*index=5*/s32[]{:T(128)}, s32[]{:T(128)}, s32[]{:T(128)}) while((s32[]{:T(128)}, f32[8,2,2,4,2048]{4,3,2,1,0:T(4,128)}, s32[8]{0:T(128)S(1)}, f32[2,4,256]{2,1,0:T(4,128)S(1)}, ...), condition=%wide.region_1.2_spmd.clone, body=%wide.region_0.1_spmd.clone.sunk | while | flops 207937696 | bytes 28771064 | solution.py:131
  136.4 1.9 multiply_cosine_fusion.6
  140.6 1.2 fusion.167
  141.8 1.2 fusion.168
  143.0 1.2 fusion.169
  147.2 1.2 fusion.172
  148.4 1.2 fusion.173
  151.7 1.9 multiply_cosine_fusion.6
  155.9 1.2 fusion.167
  157.1 1.2 fusion.168
  158.3 1.2 fusion.169
  161.3 1.2 fusion.171
  162.5 1.2 fusion.172
  163.7 1.2 fusion.173
  167.0 1.9 multiply_cosine_fusion.6
  171.2 1.2 fusion.167
  172.4 1.2 fusion.168
  173.6 1.2 fusion.169
  176.6 1.2 fusion.171
  177.8 1.2 fusion.172
  179.0 1.2 fusion.173
  182.3 1.9 multiply_cosine_fusion.6
  186.5 1.2 fusion.167
  187.7 1.2 fusion.168
  191.9 1.2 fusion.171
  193.1 1.2 fusion.172
  197.6 1.9 multiply_cosine_fusion.6
  203.0 1.2 fusion.168
  208.4 1.2 fusion.172
  212.9 1.9 multiply_cosine_fusion.6
  218.3 1.2 fusion.168
  223.7 1.2 fusion.172
  228.2 1.9 multiply_cosine_fusion.6
  233.6 1.2 fusion.168
  239.0 1.2 fusion.172
  243.5 1.9 multiply_cosine_fusion.6
  248.9 1.2 fusion.168
  254.3 1.2 fusion.172
  257.4 2.4 copy.16
  259.9 12.3 %fusion.89 = (f32[1,8,32,512]{3,2,1,0:T(8,128)S(1)}, f32[8,32,512]{2,1,0:T(8,128)S(1)}) fusion(f32[8,32,512]{2,1,0:T(8,128)S(1)} %copy-done.11, f32[8,32,512]{2,1,0:T(8,128)S(1)} %get-tuple-element.178, f32[7,32,512]{2,1,0:T(8,128)} %slice.458, f32[1,32,512]{2,1,0:T(8,128)S(1)} %get-tuple-element.180, f32[8,32,512]{2,1,0:T(8,128)S(1)} %get-tuple-element.176, ...), kind=kLoop, calls=%fused_computation.139 | loop fusion | flops 5636096 | bytes 5242944 | tf_op jit(solution)/shard_map/stack | solution.py:197
  272.2 1.3 pad_maximum_fusion
  273.7 1.3 pad_maximum_fusion.2
  275.0 115.0 %all-reduce.10.cloned.1.call-done = f32[2,2,4,16384]{3,2,1,0:T(4,128)} async-done(((f32[2,2,4,16384]{3,2,1,0:T(4,128)}), f32[2,2,4,16384]{3,2,1,0:T(4,128)}) %all-reduce.10.cloned.1.call-update) | async-done | bytes 1048592 | tf_op jit(solution)/shard_map/psum | solution.py:193
  389.9 2.5 broadcast_multiply_fusion
  (263 shorter events, 96.3 us)
Async XLA Ops:
  7.2 3.1 copy-start
  7.2 5.5 %copy-start.33 = (f32[4]{0:T(128)S(1)}, f32[4]{0:T(128)}, u32[]{:S(2)}) copy-start(f32[4]{0:T(128)} %param.17) | copy-start | bytes 52
  7.2 6.2 %copy-start.30 = (f32[4]{0:T(128)S(1)}, f32[4]{0:T(128)}, u32[]{:S(2)}) copy-start(f32[4]{0:T(128)} %param.19) | copy-start | bytes 52
  7.2 6.1 %copy-start.31 = (f32[4]{0:T(128)S(1)}, f32[4]{0:T(128)}, u32[]{:S(2)}) copy-start(f32[4]{0:T(128)} %param.20) | copy-start | bytes 52
  7.2 6.1 %copy-start.32 = (f32[4]{0:T(128)S(1)}, f32[4]{0:T(128)}, u32[]{:S(2)}) copy-start(f32[4]{0:T(128)} %param.18) | copy-start | bytes 52
  7.2 382.7 %all-reduce.10.cloned.1.call-start = ((), (), s32[]{:S(2)}) async-start(), calls=%async_computation | async-start | bytes 2097152 | tf_op jit(solution)/shard_map/psum | solution.py:193
  9.0 10.7 %collective-permute-start.1 = (f32[2,8,1,512]{3,2,1,0:T(1,128)S(1)}, f32[2,8,1,512]{3,2,1,0:T(1,128)S(1)}, u32[]{:S(2)}, u32[]{:S(2)}) collective-permute-start(f32[2,8,1,512]{3,2,1,0:T(1,128)S(1)} %pad_maximum_fusion.6), channel_id=1, source_target_pairs={{1,0},{2,1},{3,2},{4,3},{5,4},{6,5},{7,6},{9,8},{10,9},{11,10},{12... | collective-permute-start | bytes 98312 | tf_op jit(solution)/shard_map/ppermute | solution.py:21
  10.3 9.4 %collective-permute-start = (f32[2,1,32,512]{3,2,1,0:T(8,128)S(1)}, f32[2,1,32,512]{3,2,1,0:T(8,128)S(1)}, u32[]{:S(2)}, u32[]{:S(2)}) collective-permute-start(f32[2,1,32,512]{3,2,1,0:T(8,128)S(1)} %stack.204), channel_id=1, source_target_pairs={{8,0},{16,8},{24,16},{9,1},{17,9},{25,17},{10,2},{18,10},{26,18},{... | collective-permute-start | bytes 393224 | tf_op jit(solution)/shard_map/ppermute | solution.py:21
  23.1 12.8 %collective-permute-start.2 = (f32[2,8,1,512]{3,2,1,0:T(1,128)S(1)}, f32[2,8,1,512]{3,2,1,0:T(1,128)S(1)}, u32[]{:S(2)}, u32[]{:S(2)}) collective-permute-start(f32[2,8,1,512]{3,2,1,0:T(1,128)S(1)} %pad_maximum_fusion.7), channel_id=1, source_target_pairs={{0,1},{1,2},{2,3},{3,4},{4,5},{5,6},{6,7},{8,9},{9,10},{10,11},{11... | collective-permute-start | bytes 98312 | tf_op jit(solution)/shard_map/ppermute | solution.py:21
  28.5 25.5 %collective-permute-start.3 = (f32[2,1,32,512]{3,2,1,0:T(8,128)}, f32[2,1,32,512]{3,2,1,0:T(8,128)}, u32[]{:S(2)}, u32[]{:S(2)}) collective-permute-start(f32[2,1,32,512]{3,2,1,0:T(8,128)} %pad_maximum_fusion.3), channel_id=1, source_target_pairs={{0,8},{8,16},{16,24},{1,9},{9,17},{17,25},{2,10},{10,18},{18,26},{... | collective-permute-start | bytes 393224 | tf_op jit(solution)/shard_map/ppermute | solution.py:21
  49.1 1.9 copy-start.1
  54.8 13.9 %copy-start.12 = (pred[8,32,512]{2,1,0:T(8,128)(4,1)S(1)}, pred[8,32,512]{2,1,0:T(8,128)(4,1)}, u32[]{:S(2)}) copy-start(pred[8,32,512]{2,1,0:T(8,128)(4,1)} %get-tuple-element.141) | copy-start | bytes 393220
  54.8 13.9 %copy-start.22 = (f32[7,32,512]{2,1,0:T(8,128)S(1)}, f32[7,32,512]{2,1,0:T(8,128)}, u32[]{:S(2)}) copy-start(f32[7,32,512]{2,1,0:T(8,128)} %slice.428) | copy-start | bytes 1376260
  67.9 0.8 copy-start.8
  68.7 16.2 %copy-start.27 = (f32[1,1,256]{2,1,0:T(1,128)S(1)}, f32[1,1,256]{2,1,0:T(1,128)}, u32[]{:S(2)}) copy-start(f32[1,1,256]{2,1,0:T(1,128)} %stack.239) | copy-start | bytes 3076
  68.7 16.2 %copy-start.28 = (f32[1,1,256]{2,1,0:T(1,128)S(1)}, f32[1,1,256]{2,1,0:T(1,128)}, u32[]{:S(2)}) copy-start(f32[1,1,256]{2,1,0:T(1,128)} %stack.238) | copy-start | bytes 3076
  68.7 16.2 %copy-start.29 = (f32[1,1,256]{2,1,0:T(1,128)S(1)}, f32[1,1,256]{2,1,0:T(1,128)}, u32[]{:S(2)}) copy-start(f32[1,1,256]{2,1,0:T(1,128)} %stack.241) | copy-start | bytes 3076
  81.5 0.8 copy-start.4
  81.5 6.6 %copy-start.9 = (f32[8,32,512]{2,1,0:T(8,128)S(1)}, f32[8,32,512]{2,1,0:T(8,128)}, u32[]{:S(2)}) copy-start(f32[8,32,512]{2,1,0:T(8,128)} %copy-done.8) | copy-start | bytes 1572868
  82.5 5.6 %copy-start.5 = (f32[8,32,512]{2,1,0:T(8,128)S(1)}, f32[8,32,512]{2,1,0:T(8,128)}, u32[]{:S(2)}) copy-start(f32[8,32,512]{2,1,0:T(8,128)} %copy-done.4) | copy-start | bytes 1572868
  82.5 7.0 %collective-permute-start.5 = (f32[2,8,1,512]{3,2,1,0:T(1,128)S(1)}, f32[2,8,1,512]{3,2,1,0:T(1,128)S(1)}, u32[]{:S(2)}, u32[]{:S(2)}) collective-permute-start(f32[2,8,1,512]{3,2,1,0:T(1,128)S(1)} %pad_maximum_fusion.8), channel_id=1, source_target_pairs={{1,0},{2,1},{3,2},{4,3},{5,4},{6,5},{7,6},{9,8},{10,9},{11,10},{12... | collective-permute-start | bytes 98312 | tf_op jit(solution)/shard_map/ppermute | solution.py:21
  85.5 9.8 %copy-start.2 = (f32[8,32,512]{2,1,0:T(8,128)S(1)}, f32[8,32,512]{2,1,0:T(8,128)}, u32[]{:S(2)}) copy-start(f32[8,32,512]{2,1,0:T(8,128)} %copy-done.1) | copy-start | bytes 1572868
  85.5 9.8 %copy-start.6 = (f32[8,32,512]{2,1,0:T(8,128)S(1)}, f32[8,32,512]{2,1,0:T(8,128)}, u32[]{:S(2)}) copy-start(f32[8,32,512]{2,1,0:T(8,128)} %copy-done.4) | copy-start | bytes 1572868
  85.5 9.8 %copy-start.10 = (f32[8,32,512]{2,1,0:T(8,128)S(1)}, f32[8,32,512]{2,1,0:T(8,128)}, u32[]{:S(2)}) copy-start(f32[8,32,512]{2,1,0:T(8,128)} %copy-done.8) | copy-start | bytes 1572868
  85.5 9.8 %copy-start.20 = (f32[8,31,512]{2,1,0:T(8,128)S(1)}, f32[8,31,512]{2,1,0:T(8,128)}, u32[]{:S(2)}) copy-start(f32[8,31,512]{2,1,0:T(8,128)} %slice.437) | copy-start | bytes 1523716
  85.6 9.8 %copy-start.21 = (f32[8,32,511]{2,1,0:T(8,128)S(1)}, f32[8,32,511]{2,1,0:T(8,128)}, u32[]{:S(2)}) copy-start(f32[8,32,511]{2,1,0:T(8,128)} %slice.448) | copy-start | bytes 1569796
  88.2 7.1 %collective-permute-start.4 = (f32[2,1,32,512]{3,2,1,0:T(8,128)S(1)}, f32[2,1,32,512]{3,2,1,0:T(8,128)S(1)}, u32[]{:S(2)}, u32[]{:S(2)}) collective-permute-start(f32[2,1,32,512]{3,2,1,0:T(8,128)S(1)} %pad_maximum_fusion.4), channel_id=1, source_target_pairs={{8,0},{16,8},{24,16},{9,1},{17,9},{25,17},{10,2},{18,10},{26,18},{... | collective-permute-start | bytes 393224 | tf_op jit(solution)/shard_map/ppermute | solution.py:21
  96.5 10.8 %collective-permute-start.6 = (f32[2,8,1,512]{3,2,1,0:T(1,128)S(1)}, f32[2,8,1,512]{3,2,1,0:T(1,128)S(1)}, u32[]{:S(2)}, u32[]{:S(2)}) collective-permute-start(f32[2,8,1,512]{3,2,1,0:T(1,128)S(1)} %pad_maximum_fusion.9), channel_id=1, source_target_pairs={{0,1},{1,2},{2,3},{3,4},{4,5},{5,6},{6,7},{8,9},{9,10},{10,11},{11... | collective-permute-start | bytes 98312 | tf_op jit(solution)/shard_map/ppermute | solution.py:21
  99.4 7.9 %copy-start.3 = (f32[8,32,512]{2,1,0:T(8,128)S(1)}, f32[8,32,512]{2,1,0:T(8,128)}, u32[]{:S(2)}) copy-start(f32[8,32,512]{2,1,0:T(8,128)} %copy-done.1) | copy-start | bytes 1572868
  99.4 7.9 %copy-start.13 = (pred[8,32,512]{2,1,0:T(8,128)(4,1)S(1)}, pred[8,32,512]{2,1,0:T(8,128)(4,1)}, u32[]{:S(2)}) copy-start(pred[8,32,512]{2,1,0:T(8,128)(4,1)} %get-tuple-element.141) | copy-start | bytes 393220
  102.3 18.9 %collective-permute-start.7 = (f32[2,1,32,512]{3,2,1,0:T(8,128)S(1)}, f32[2,1,32,512]{3,2,1,0:T(8,128)S(1)}, u32[]{:S(2)}, u32[]{:S(2)}) collective-permute-start(f32[2,1,32,512]{3,2,1,0:T(8,128)S(1)} %pad_maximum_fusion.5), channel_id=1, source_target_pairs={{0,8},{8,16},{16,24},{1,9},{9,17},{17,25},{2,10},{10,18},{18,26},{... | collective-permute-start | bytes 393224 | tf_op jit(solution)/shard_map/ppermute | solution.py:21
  107.3 13.9 %copy-start.7 = (f32[8,32,512]{2,1,0:T(8,128)S(1)}, f32[8,32,512]{2,1,0:T(8,128)}, u32[]{:S(2)}) copy-start(f32[8,32,512]{2,1,0:T(8,128)} %copy-done.4) | copy-start | bytes 1572868
  120.2 0.8 copy-start.14
  121.2 13.2 %copy-start.25 = (f32[1,4,256]{2,1,0:T(4,128)S(1)}, f32[1,4,256]{2,1,0:T(4,128)}, u32[]{:S(2)}) copy-start(f32[1,4,256]{2,1,0:T(4,128)} %get-tuple-element.200) | copy-start | bytes 12292
  121.2 13.2 %copy-start.26 = (f32[1,4,256]{2,1,0:T(4,128)S(1)}, f32[1,4,256]{2,1,0:T(4,128)}, u32[]{:S(2)}) copy-start(f32[1,4,256]{2,1,0:T(4,128)} %get-tuple-element.202) | copy-start | bytes 12292
  121.2 13.2 %copy-start.23 = (f32[1,4,256]{2,1,0:T(4,128)S(1)}, f32[1,4,256]{2,1,0:T(4,128)}, u32[]{:S(2)}) copy-start(f32[1,4,256]{2,1,0:T(4,128)} %get-tuple-element.199) | copy-start | bytes 12292
  121.3 13.2 %copy-start.24 = (f32[1,4,256]{2,1,0:T(4,128)S(1)}, f32[1,4,256]{2,1,0:T(4,128)}, u32[]{:S(2)}) copy-start(f32[1,4,256]{2,1,0:T(4,128)} %get-tuple-element.201) | copy-start | bytes 12292
  121.3 13.2 %copy-start.34 = (s32[8]{0:T(128)S(1)}, s32[8]{0:T(128)}, u32[]{:S(2)}) copy-start(s32[8]{0:T(128)} %iota_multiply_fusion) | copy-start | bytes 100
  134.2 0.8 copy-start.16
  257.4 2.5 copy-start.11
  259.9 12.3 %copy-start.15 = (f32[8,32,512]{2,1,0:T(8,128)S(1)}, f32[8,32,512]{2,1,0:T(8,128)}, u32[]{:S(2)}) copy-start(f32[8,32,512]{2,1,0:T(8,128)} %copy-done.14) | copy-start | bytes 1572868
  259.9 12.3 %copy-start.17 = (f32[8,32,512]{2,1,0:T(8,128)S(1)}, f32[8,32,512]{2,1,0:T(8,128)}, u32[]{:S(2)}) copy-start(f32[8,32,512]{2,1,0:T(8,128)} %copy-done.16) | copy-start | bytes 1572868
  272.2 1.3 copy-start.18
  272.2 1.5 copy-start.19
Sparse Core Ops, SparseCore 0:
  260.0 129.8 all-reduce.9
where the time goes:
time: 401 us; the launch traced here: 399 us
  other arithmetic  132 us (33%)
  waiting for transfers between devices  121 us (30%)
  matrix products  76.3 us (19%)
  local copies, waits for them, and re-layouts  32.3 us (8%)
  starting transfers between devices  22.1 us (6%)
  between operations  15.5 us (4%)
    psum x1, waiting for transfers between devices, shards(): total = lax.psum(partial_far, ('gx', 'gy'))  115 us
    add x5, other arithmetic, shards(): fields[i] + (DT * curls[i] - (newpol[i] - pols[i])) * vox_inv  64.9 us
    ppermute x8, starting transfers between devices, shifted(): return lax.ppermute(shard, axis, pairs)  22.1 us
    dot_general x16, matrix products, project(): jnp.dot(real_flat[f], cosine, precision=hi)  19.1 us
    dot_general x16, matrix products, project(): jnp.dot(imag_flat[f], cosine, precision=hi)  19.1 us
    dot_general x16, matrix products, project(): jnp.dot(imag_flat[f], sine, precision=hi)  19.1 us
    dot_general x16, matrix products, project(): jnp.dot(real_flat[f], sine, precision=hi)  19 us
    cos x8, other arithmetic, project(): cos_y = jnp.cos(along_y)  15.1 us
  transfers between devices with their start and end apart: 9, of which 2 were waited for; matrix products, arithmetic and copies ran while one was open for 16% of the time, Pallas kernels for 0%

commit v1 on v0

v1 whole, which is shorter than its diff:
```python
import functools
import math

import jax
import jax.numpy as jnp
import numpy as np
from jax import lax
from jax.experimental import pallas as pl
from jax.experimental.pallas import tpu as pltpu
from jax.sharding import PartitionSpec as P

NTH = 64
NPH = 256
NDIR = 16384
ZS = 384
DT = 0.55
WAVELENGTHS = (5.0, 4.0)
MESH = pl.DeviceIdType.MESH
F32 = jnp.float32
BF16 = jnp.bfloat16
BY = 8


def step_kernel(
    ngx, ngy, nmat,
    e_in, h_in, p_in, q_in, m_in, eps, delta, omega, damping, flags,
    e_out, h_out, p_out, g_out,
    E, H, PA, PB, MAT, ystage, ye, yh, gather, G,
    in_sem, out_sem, xs_sem, xr_sem, ys_sem, yr_sem, g1s, g1r, g2s, g2r,
):
    cx, cy, nz = MAT.shape
    width = G.shape[2]
    gx = lax.axis_index("gx")
    gy = lax.axis_index("gy")

    loads = [
        pltpu.make_async_copy(e_in, E.at[:, pl.ds(0, cx)], in_sem.at[0]),
        pltpu.make_async_copy(h_in, H.at[:, pl.ds(1, cx)], in_sem.at[1]),
        pltpu.make_async_copy(p_in, PA, in_sem.at[2]),
        pltpu.make_async_copy(q_in, PB, in_sem.at[3]),
        pltpu.make_async_copy(m_in, MAT, in_sem.at[4]),
    ]
    for load in loads:
        load.start()

    barrier = pltpu.get_barrier_semaphore()
    for k in range(1, ngx):
        pl.semaphore_signal(barrier, inc=1, device_id=(lax.rem(gx + k, ngx), gy), device_id_type=MESH)
    for k in range(1, ngy):
        pl.semaphore_signal(barrier, inc=1, device_id=(gx, lax.rem(gy + k, ngy)), device_id_type=MESH)

    @pl.when(gx == ngx - 1)
    def _():
        for c in (1, 2):
            E[c, cx] = jnp.zeros((cy, nz), F32)

    @pl.when(gx == 0)
    def _():
        for c in (1, 2):
            H[c, 0] = jnp.zeros((cy, nz), F32)

    @pl.when(gy == ngy - 1)
    def _():
        ye[...] = jnp.zeros(ye.shape, F32)

    @pl.when(gy == 0)
    def _():
        yh[...] = jnp.zeros(yh.shape, F32)

    def copies(rnd, step):
        if rnd % 2 == 0:
            xsrc, xdst, ydst = E.at[1:3, 0], E.at[1:3, cx], ye.at[step]
            tx, ty = gx - 1, gy - 1
            sends_x, sends_y = gx > 0, gy > 0
            takes_x, takes_y = gx < ngx - 1, gy < ngy - 1
        else:
            xsrc, xdst, ydst = H.at[1:3, cx], H.at[1:3, 0], yh.at[step]
            tx, ty = gx + 1, gy + 1
            sends_x, sends_y = gx < ngx - 1, gy < ngy - 1
            takes_x, takes_y = gx > 0, gy > 0
        xcopy = pltpu.make_async_remote_copy(
            src_ref=xsrc, dst_ref=xdst, send_sem=xs_sem.at[rnd], recv_sem=xr_sem.at[rnd],
            device_id=(lax.rem(tx + ngx, ngx), gy), device_id_type=MESH)
        ycopy = pltpu.make_async_remote_copy(
            src_ref=ystage.at[rnd], dst_ref=ydst, send_sem=ys_sem.at[rnd], recv_sem=yr_sem.at[rnd],
            device_id=(gx, lax.rem(ty + ngy, ngy)), device_id_type=MESH)
        return xcopy, ycopy, sends_x, sends_y, takes_x, takes_y

    def send_x(rnd, step):
        xcopy, _, sends_x, _, _, _ = copies(rnd, step)
        pl.when(sends_x)(xcopy.start)

    def send_y(rnd, step):
        _, ycopy, _, sends_y, _, _ = copies(rnd, step)
        for i, c in enumerate((0, 2)):
            for x in range(cx):
                if rnd % 2 == 0:
                    ystage[rnd, i, x : x + 1, :] = E[c, x, 0:1, :]
                else:
                    ystage[rnd, i, x : x + 1, :] = H[c, x + 1, cy - 1 : cy, :]
        pl.when(sends_y)(ycopy.start)

    def take_x(rnd, step):
        xcopy, _, _, _, takes_x, _ = copies(rnd, step)
        pl.when(takes_x)(xcopy.wait_recv)

    def take_y(rnd, step):
        _, ycopy, _, _, _, takes_y = copies(rnd, step)
        pl.when(takes_y)(ycopy.wait_recv)

    def sent_x(rnd, step):
        xcopy, _, sends_x, _, _, _ = copies(rnd, step)
        pl.when(sends_x)(xcopy.wait_send)

    def sent_y(rnd, step):
        _, ycopy, _, sends_y, _, _ = copies(rnd, step)
        pl.when(sends_y)(ycopy.wait_send)

    row_id = lax.broadcasted_iota(jnp.int32, (BY, nz), 0)
    lane_id = lax.broadcasted_iota(jnp.int32, (BY, nz), 1)

    def up_y(v, row):
        return jnp.where(row_id == BY - 1, row, pltpu.roll(v, BY - 1, 0))

    def up_z(v):
        return jnp.where(lane_id == nz - 1, 0.0, pltpu.roll(v, nz - 1, 1))

    def down_y(v, row):
        return jnp.where(row_id == 0, row, pltpu.roll(v, 1, 0))

    def down_z(v):
        return jnp.where(lane_id == 0, 0.0, pltpu.roll(v, 1, 1))

    def h_plane(step, x):
        for y in range(0, cy, BY):
            here = pl.ds(y, BY)
            ex, ey, ez = E[0, x, here, :], E[1, x, here, :], E[2, x, here, :]
            if y + BY < cy:
                rx, rz = E[0, x, y + BY : y + BY + 1, :], E[2, x, y + BY : y + BY + 1, :]
            else:
                rx, rz = ye[step, 0, pl.ds(x, 1), :], ye[step, 1, pl.ds(x, 1), :]
            eyx, ezx = E[1, x + 1, here, :], E[2, x + 1, here, :]
            curl_x = (up_y(ez, rz) - ez) - (up_z(ey) - ey)
            curl_y = (up_z(ex) - ex) - (ezx - ez)
            curl_z = (eyx - ey) - (up_y(ex, rx) - ex)
            H[0, x + 1, here, :] = H[0, x + 1, here, :] - DT * curl_x
            H[1, x + 1, here, :] = H[1, x + 1, here, :] - DT * curl_y
            H[2, x + 1, here, :] = H[2, x + 1, here, :] - DT * curl_z

    coef = []
    for m in range(nmat):
        half = jnp.full((1, nz), damping[m], F32) * (DT / 2.0)
        denom = 1.0 + half
        om = jnp.full((1, nz), omega[m], F32)
        square = om * om * (DT * DT)
        coef.append((
            (2.0 - square) / denom,
            (half - 1.0) / denom,
            jnp.full((1, nz), delta[m], F32) * square / denom,
            1.0 / jnp.full((1, nz), eps[m], F32),
        ))

    def e_plane(step, x):
        now, old = (PA, PB) if step == 0 else (PB, PA)
        for y in range(0, cy, BY):
            here = pl.ds(y, BY)
            mat = MAT[x, here, :]
            vox = [jnp.broadcast_to(coef[nmat - 1][i], (BY, nz)) for i in range(4)]
            for m in range(nmat - 1):
                hit = mat == m
                vox = [jnp.where(hit, coef[m][i], vox[i]) for i in range(4)]
            a, b, c, inv = vox
            hx, hy, hz = H[0, x + 1, here, :], H[1, x + 1, here, :], H[2, x + 1, here, :]
            if y > 0:
                rx, rz = H[0, x + 1, y - 1 : y, :], H[2, x + 1, y - 1 : y, :]
            else:
                rx, rz = yh[step, 0, pl.ds(x, 1), :], yh[step, 1, pl.ds(x, 1), :]
            hyx, hzx = H[1, x, here, :], H[2, x, here, :]
            curls = (
                (hz - down_y(hz, rz)) - (hy - down_z(hy)),
                (hx - down_z(hx)) - (hz - hzx),
                (hy - hyx) - (hx - down_y(hx, rx)),
            )
            for i in range(3):
                e, p = E[i, x, here, :], now[i, x, here, :]
                new = a * p + b * old[i, x, here, :] + c * e
                E[i, x, here, :] = e + (DT * curls[i] - (new - p)) * inv
                old[i, x, here, :] = new

    flag = flags[0, 0].astype(F32)
    surf_lane = lax.broadcasted_iota(jnp.int32, (cy, width), 1)

    def surface(step):
        def body(x, acc):
            base = (gx * cx + x) * 4
            cols = (
                -H[1, x + 1, :, ZS : ZS + 1], H[0, x + 1, :, ZS : ZS + 1],
                E[1, x, :, ZS : ZS + 1], -E[0, x, :, ZS : ZS + 1],
            )
            for j in range(4):
                acc = jnp.where(surf_lane == base + j, cols[j] * flag, acc)
            return acc

        gather[step, gx] = lax.fori_loop(0, cx, body, jnp.zeros((cy, width), F32))

    def first(step, k):
        return pltpu.make_async_remote_copy(
            src_ref=gather.at[step, gx], dst_ref=gather.at[step, gx],
            send_sem=g1s.at[step, k], recv_sem=g1r.at[step, k],
            device_id=(lax.rem(gx + k, ngx), gy), device_id_type=MESH)

    def second(step, k):
        rows = pl.ds(pl.multiple_of(gy * cy, cy), cy)
        return pltpu.make_async_remote_copy(
            src_ref=G.at[step, rows], dst_ref=G.at[step, rows],
            send_sem=g2s.at[step, k], recv_sem=g2r.at[step, k],
            device_id=(gx, lax.rem(gy + k, ngy)), device_id_type=MESH)

    def gather_first(step):
        for k in range(1, ngx):
            first(step, k).start()

    def gather_second(step):
        for k in range(1, ngx):
            first(step, k).wait()
        total = gather[step, 0]
        for i in range(1, ngx):
            total = total + gather[step, i]
        G[step, pl.ds(pl.multiple_of(gy * cy, cy), cy)] = total
        for k in range(1, ngy):
            second(step, k).start()

    def gather_end(step):
        for k in range(1, ngy):
            second(step, k).wait()

    loads[0].wait()
    pl.semaphore_wait(barrier, ngx + ngy - 2)
    send_x(0, 0)
    send_y(0, 0)
    loads[1].wait()

    for step in range(2):
        down, up = 2 * step, 2 * step + 1
        take_y(down, step)

        @pl.loop(0, cx - 1)
        def _(x):
            h_plane(step, x)

        take_x(down, step)
        h_plane(step, cx - 1)
        send_x(up, step)
        send_y(up, step)
        if step == 0:
            for load in loads[2:]:
                load.wait()
        else:
            pltpu.make_async_copy(H.at[:, pl.ds(1, cx)], h_out, out_sem.at[0]).start()
            gather_second(0)
        sent_x(down, step)
        take_y(up, step)

        @pl.loop(1, cx)
        def _(x):
            e_plane(step, x)

        take_x(up, step)
        e_plane(step, 0)
        if step == 0:
            send_x(2, 1)
            send_y(2, 1)
            sent_x(up, step)
        surface(step)
        gather_first(step)

    saves = [
        pltpu.make_async_copy(H.at[:, pl.ds(1, cx)], h_out, out_sem.at[0]),
        pltpu.make_async_copy(E.at[:, pl.ds(0, cx)], e_out, out_sem.at[1]),
        pltpu.make_async_copy(PA, p_out, out_sem.at[2]),
    ]
    saves[1].start()
    saves[2].start()
    gather_end(0)
    gather_second(1)
    gather_end(1)
    last = pltpu.make_async_copy(G, g_out, out_sem.at[3])
    last.start()
    sent_x(3, 1)
    for rnd in range(4):
        sent_y(rnd, rnd // 2)
    for save in saves:
        save.wait()
    last.wait()


def make_seeds():
    theta = (np.arange(NTH, dtype=np.float64)[:, None] + 0.5) * (math.pi / 2.0 / NTH)
    phi = (np.arange(NPH // 4, dtype=np.float64)[None, :] + 0.5) * (2.0 * math.pi / NPH)
    ux = (np.sin(theta) * np.cos(phi)).reshape(-1)
    uy = (np.sin(theta) * np.sin(phi)).reshape(-1)
    rows = []
    for length in WAVELENGTHS:
        wave = 2.0 * math.pi / length
        for angle in (uy, 8.0 * uy, ux, 2.0 * ux):
            rows += [np.cos(wave * angle), np.sin(wave * angle)]
    return np.stack(rows).astype(np.float32)


def make_spread():
    spread = np.zeros((256, 256), np.float32)
    for r in range(256):
        t, p = (r % 128) // 64, r % 64
        spread[r, t * 128 + (p if r < 128 else 127 - p)] = 1.0
    return spread


TILE = 512


def far_kernel(
    nx, ny, g_ref, seeds, spread, e_in, h_in, p_in, far, e_out, h_out, p_out,
    a_wide, a_low, t_cos, t_sin, s_cos, s_sin, packed, sem,
):
    pid = pl.program_id(0)
    width = 4 * nx
    saves = [
        pltpu.make_async_copy(src, dst, sem.at[i])
        for i, (src, dst) in enumerate(((e_in, e_out), (h_in, h_out), (p_in, p_out)))
    ]

    @pl.when(pid == 0)
    def _():
        for save in saves:
            save.start()
        for s in range(2):
            a = g_ref[s].T
            high = a.astype(BF16)
            rows = pl.ds(s * width, width)
            a_wide[rows, 0:ny] = high
            a_wide[rows, ny : 2 * ny] = high
            a_low[rows, :] = (a - high.astype(F32)).astype(BF16)

    scale = 1.0 / math.sqrt(nx * ny)
    part = 256
    sub = lax.broadcasted_iota(jnp.int32, (8, part), 0)
    for f in range(2):
        omega = 2.0 * math.pi / WAVELENGTHS[f]
        kappa = [math.cos(omega * (s + 1) * DT) * scale for s in range(2)]
        sigma = [math.sin(omega * (s + 1) * DT) * scale for s in range(2)]

        def seed(i, lanes):
            row = 8 * f + i
            return jnp.broadcast_to(seeds[row : row + 1, lanes], (8, part))

        def times(a, b):
            return (a[0] * b[0] - a[1] * b[1], a[0] * b[1] + a[1] * b[0])

        one = jnp.ones((8, part), F32)
        zero = jnp.zeros((8, part), F32)

        def chosen(bit, z):
            on = (sub & bit) != 0
            return (jnp.where(on, z[0], one), jnp.where(on, z[1], zero))

        for o in range(0, TILE, part):
            lanes = slice(o, o + part)
            e1 = (seed(0, lanes), seed(1, lanes))
            e8 = (seed(2, lanes), seed(3, lanes))
            e2 = times(e1, e1)
            e4 = times(e2, e2)
            v = times(times(chosen(1, e1), chosen(2, e2)), chosen(4, e4))
            e16 = times(e8, e8)
            w = times(v, e8)

            def fill(k, carry):
                v, w = (carry[0], carry[1]), (carry[2], carry[3])
                at = pl.multiple_of(k * 16, 16)
                for i, table in ((0, t_cos), (1, t_sin)):
                    full = jnp.concatenate([v[i], w[i]], axis=0)
                    high = full.astype(BF16)
                    table[pl.ds(at, 16), lanes] = high
                    table[pl.ds(pl.multiple_of(at + ny, 16), 16), lanes] = (full - high.astype(F32)).astype(BF16)
                return times(v, e16) + times(w, e16)

            lax.fori_loop(0, ny // 16, fill, v + w, unroll=4)

        for table, result in ((t_cos, s_cos), (t_sin, s_sin)):
            result[...] = jnp.dot(a_wide[...], table[...], preferred_element_type=F32) + jnp.dot(
                a_low[...], table[0:ny, :], preferred_element_type=F32)

        for o in range(0, TILE, part):
            lanes = slice(o, o + part)
            w0 = chosen(4, (seed(4, lanes), seed(5, lanes)))
            e2 = (seed(6, lanes), seed(7, lanes))

            def add(k, carry):
                w, sums = (carry[0], carry[1]), carry[2:]
                fresh = []
                for s in range(2):
                    rows = pl.ds(pl.multiple_of(s * width + k * 8, 8), 8)
                    c, d = s_cos[rows, lanes], s_sin[rows, lanes]
                    fresh += [c * w[0], c * w[1], d * w[0], d * w[1]]
                return times(w, e2) + tuple(t + n for t, n in zip(sums, fresh))

            out = lax.fori_loop(0, nx // 2, add, w0 + (zero,) * 8, unroll=4)
            sums = out[2:]
            re = [zero] * 4
            im = [zero] * 4
            for s in range(2):
                cc, cs, sc, ss = sums[4 * s : 4 * s + 4]
                a, b, c, d = cc - ss, cs + sc, cc + ss, sc - cs
                k, g = kappa[s], sigma[s]
                re[0] += a * k + b * g
                im[0] += b * k - a * g
                re[1] += c * k + d * g
                im[1] += d * k - c * g
                re[2] += a * k - b * g
                im[2] -= b * k + a * g
                re[3] += c * k - d * g
                im[3] -= d * k + c * g
            for q in range(4):
                r = re[q] + pltpu.roll(re[q], 4, 0)
                i = im[q] + pltpu.roll(im[q], 4, 0)
                both = jnp.where(sub < 4, r, i)
                for pair in range(part // 128):
                    at = (((o // 128 + pair) * 2 + f) * 2 + q // 2) * 8
                    packed[at : at + 8, (q % 2) * 128 : (q % 2) * 128 + 128] = both[:, pair * 128 : pair * 128 + 128]

    done = jnp.dot(packed[...], spread[...], precision=lax.Precision.HIGHEST, preferred_element_type=F32)
    for pair in range(TILE // 128):
        for f in range(2):
            for h in range(2):
                at = ((pair * 2 + f) * 2 + h) * 8
                for t in range(2):
                    d = (2 * pair + t) * 256 + h * 128
                    far[f, 0, :, d : d + 128] = done[at : at + 4, t * 128 : t * 128 + 128]
                    far[f, 1, :, d : d + 128] = done[at + 4 : at + 8, t * 128 : t * 128 + 128]

    @pl.when(pid == pl.num_programs(0) - 1)
    def _():
        for save in saves:
            save.wait()


def shards(
    e_field, h_field, polar, polar_prev, material,
    eps_table, delta_table, omega_table, damping_table, surface_flags,
):
    _, cx, cy, nz = e_field.shape
    ngx, ngy = lax.axis_size("gx"), lax.axis_size("gy")
    nx, ny = ngx * cx, ngy * cy
    width = 4 * nx
    hbm = pl.BlockSpec(memory_space=pl.ANY)
    smem = pl.BlockSpec(memory_space=pltpu.SMEM)
    field = jax.ShapeDtypeStruct(e_field.shape, F32)
    dma = pltpu.SemaphoreType.DMA
    e, h, p, g = pl.pallas_call(
        functools.partial(step_kernel, ngx, ngy, eps_table.shape[0]),
        out_shape=(field, field, field, jax.ShapeDtypeStruct((2, ny, width), F32)),
        in_specs=[hbm] * 5 + [smem] * 5,
        out_specs=(hbm,) * 4,
        scratch_shapes=[
            pltpu.VMEM((3, cx + 1, cy, nz), F32),
            pltpu.VMEM((3, cx + 1, cy, nz), F32),
            pltpu.VMEM((3, cx, cy, nz), F32),
            pltpu.VMEM((3, cx, cy, nz), F32),
            pltpu.VMEM((cx, cy, nz), jnp.int32),
            pltpu.VMEM((4, 2, cx, nz), F32),
            pltpu.VMEM((2, 2, cx, nz), F32),
            pltpu.VMEM((2, 2, cx, nz), F32),
            pltpu.VMEM((2, ngx, cy, width), F32),
            pltpu.VMEM((2, ny, width), F32),
            dma((5,)), dma((4,)), dma((4,)), dma((4,)), dma((4,)), dma((4,)),
            dma((2, ngx)), dma((2, ngx)), dma((2, ngy)), dma((2, ngy)),
        ],
        compiler_params=pltpu.CompilerParams(
            collective_id=0, has_side_effects=True, vmem_limit_bytes=24 * 1024 * 1024),
    )(e_field, h_field, polar, polar_prev, material,
      eps_table, delta_table, omega_table, damping_table, surface_flags)

    steps = (NDIR // 4) // TILE
    whole = lambda *shape: pl.BlockSpec(shape, lambda i: (0,) * len(shape))
    far, e, h, p = pl.pallas_call(
        functools.partial(far_kernel, nx, ny),
        grid=(steps,),
        out_shape=(jax.ShapeDtypeStruct((2, 2, 4, NDIR), F32), field, field, field),
        in_specs=[
            whole(2, ny, width),
            pl.BlockSpec((16, TILE), lambda i: (0, i)),
            whole(256, 256),
            hbm, hbm, hbm,
        ],
        out_specs=(pl.BlockSpec((2, 2, 4, 4 * TILE), lambda i: (0, 0, 0, i)), hbm, hbm, hbm),
        scratch_shapes=[
            pltpu.VMEM((2 * width, 2 * ny), BF16),
            pltpu.VMEM((2 * width, ny), BF16),
            pltpu.VMEM((2 * ny, TILE), BF16),
            pltpu.VMEM((2 * ny, TILE), BF16),
            pltpu.VMEM((2 * width, TILE), F32),
            pltpu.VMEM((2 * width, TILE), F32),
            pltpu.VMEM((4 * (TILE // 128) * 8, 256), F32),
            dma((3,)),
        ],
        compiler_params=pltpu.CompilerParams(vmem_limit_bytes=32 * 1024 * 1024),
    )(g, jnp.asarray(make_seeds()), jnp.asarray(make_spread()), e, h, p)
    return e, h, p, far


def solution(mesh):
    cells = P(None, "gx", "gy", None)
    placed = (cells, cells, cells, cells, P("gx", "gy", None), P(), P(), P(), P(), P("gx", "gy"))
    return jax.shard_map(
        shards, mesh=mesh, in_specs=placed, out_specs=(cells, cells, cells, P()), check_vma=False,
    )
```

time: 401 us -> 67.2 us (0.17)
  other arithmetic: 132 us -> 0 us
  waiting for transfers between devices: 121 us -> 0 us
  matrix products: 76.3 us -> 0 us
  Pallas kernels: 0 us -> 56.2 us
  local copies, waits for them, and re-layouts: 32.3 us -> 9.29 us
  starting transfers between devices: 22.1 us -> 0 us
  between operations: 15.5 us -> 1.32 us
    psum x1 -> x0, waiting for transfers between devices: 115 us -> none  [shards(): total = lax.psum(partial_far, ('gx', 'gy'))]
    dot_general x64 -> x0, matrix products: 76.3 us -> none  [the longest x16 19.1 us: project(): jnp.dot(real_flat[f], cosine, precision=hi)]
    add x6 -> x0, other arithmetic: 64.9 us -> none  [the longest x5 64.9 us: shards(): fields[i] + (DT * curls[i] - (newpol[i] - pols[i])) * vox_inv]
    pallas_call x0 -> x2, Pallas kernels: none -> 56.2 us  [the longest x1 33.3 us: shards(): pl.pallas_call(functools.partial(step_kernel, ngx, ngy, eps_table.shape[0...]
    ppermute x8 -> x0, starting transfers between devices: 22.1 us -> none  [shifted(): return lax.ppermute(shard, axis, pairs)]
    cos x16 -> x0, other arithmetic: 19.4 us -> none  [the longest x8 15.1 us: project(): cos_y = jnp.cos(along_y)]
    another operation x27 -> x0, other arithmetic: 18.1 us -> none  [the longest x2 13.6 us: shards(): jnp.stack([ex, ey, ez])]
    slice x22 -> x0, local copies, waits for them, and re-layouts: 15 us -> none  [the longest x11 9.32 us: ahead(): rest = lax.slice_in_dim(field, 1, field.shape[axis], axis=axis)]
  transfers between devices with their start and end apart: 9 -> 0, of which waited for: 2 -> 0; matrix products, arithmetic and copies ran while one was open for 16% -> 0% of each run, Pallas kernels for 0% -> 0%
where the time goes in v1:
time: 67.2 us; the launch traced here: 66.8 us
  Pallas kernels  56.2 us (84%)
  local copies, waits for them, and re-layouts  9.29 us (14%)
  between operations  1.32 us (2%)
    pallas_call x1, Pallas kernels, shards(): pl.pallas_call(functools.partial(step_kernel, ngx, ngy, eps_table.shape[0...  33.3 us
    pallas_call x1, Pallas kernels, shards(): pl.pallas_call(functools.partial(far_kernel, nx, ny), grid=(steps,), out_...  22.9 us
    unnamed x22, local copies, waits for them, and re-layouts  9.29 us

profile of v1, /device:TPU:0, one launch (start us, length us, event | category | flops | bytes accessed | tf_op | source)
XLA Modules:
  0.0 66.8 jit_solution(10468284209392863589)
XLA Ops:
  1.3 0.0 copy-start
  1.3 1.4 %copy-done = f32[3,8,32,512]{3,2,1,0:T(8,128)S(1)} copy-done((f32[3,8,32,512]{3,2,1,0:T(8,128)S(1)}, f32[3,8,32,512]{3,2,1,0:T(8,128)}, u32[]{:S(2)}) %copy-start) | copy-done | bytes 1572888
  2.7 0.0 copy-start.1
  2.7 1.4 %copy-done.1 = f32[3,8,32,512]{3,2,1,0:T(8,128)S(1)} copy-done((f32[3,8,32,512]{3,2,1,0:T(8,128)S(1)}, f32[3,8,32,512]{3,2,1,0:T(8,128)}, u32[]{:S(2)}) %copy-start.1) | copy-done | bytes 1572888
  4.1 0.0 copy-start.2
  4.1 1.4 %copy-done.2 = f32[3,8,32,512]{3,2,1,0:T(8,128)S(1)} copy-done((f32[3,8,32,512]{3,2,1,0:T(8,128)S(1)}, f32[3,8,32,512]{3,2,1,0:T(8,128)}, u32[]{:S(2)}) %copy-start.2) | copy-done | bytes 1572888
  5.5 0.0 copy-start.3
  5.5 1.4 %copy-done.3 = f32[3,8,32,512]{3,2,1,0:T(8,128)S(1)} copy-done((f32[3,8,32,512]{3,2,1,0:T(8,128)S(1)}, f32[3,8,32,512]{3,2,1,0:T(8,128)}, u32[]{:S(2)}) %copy-start.3) | copy-done | bytes 1572888
  6.9 0.0 copy-start.4
  6.9 1.0 %copy-done.4 = s32[8,32,512]{2,1,0:T(8,128)S(1)} copy-done((s32[8,32,512]{2,1,0:T(8,128)S(1)}, s32[8,32,512]{2,1,0:T(8,128)}, u32[]{:S(2)}) %copy-start.4) | copy-done | bytes 524312
  8.0 0.0 copy-start.7
  8.0 0.7 copy-done.7
  8.6 0.0 copy-start.8
  8.6 0.7 copy-done.8
  9.3 0.0 copy-start.9
  9.3 0.7 copy-done.9
  9.9 0.0 copy-start.10
  9.9 0.7 copy-done.10
  10.6 0.0 copy-start.5
  10.6 0.0 copy-start.6
  10.6 33.3 %shard_map.147 = (f32[3,8,32,512]{3,2,1,0:T(8,128)S(1)}, f32[3,8,32,512]{3,2,1,0:T(8,128)S(1)}, f32[3,8,32,512]{3,2,1,0:T(8,128)S(1)}, f32[2,256,128]{2,1,0:T(8,128)S(1)}) custom-call(f32[3,8,32,512]{3,2,1,0:T(8,128)S(1)} %copy-done, f32[3,8,32,512]{3,2,1,0:T(8,128)S(1)} %copy-done.1, f32[3,8,32,512]{3,2,1,0:T(8,128)S(1)} %copy-done.2, ...), custom_call_target="tpu_custom_call" | custom-call | tf_op jit(solution)/shard_map/pallas_call | solution.py:458
  43.9 0.0 copy-done.5
  43.9 0.0 copy-done.6
  43.9 22.9 %shard_map.148 = (f32[2,2,4,16384]{3,2,1,0:T(4,128)}, f32[3,8,32,512]{3,2,1,0:T(8,128)}, f32[3,8,32,512]{3,2,1,0:T(8,128)}, f32[3,8,32,512]{3,2,1,0:T(8,128)}) custom-call(f32[2,256,128]{2,1,0:T(8,128)S(1)} %get-tuple-element.12.g_ref, f32[16,4096]{1,0:T(8,128)S(1)} %copy-done.6, f32[256,256]{1,0:T(8,128)S(1)} %copy-done.5, ...), custom_call_target="tpu_custom_call" | custom-call | tf_op jit(solution)/shard_map/pallas_call | solution.py:484
Async XLA Ops:
  1.3 1.4 %copy-start = (f32[3,8,32,512]{3,2,1,0:T(8,128)S(1)}, f32[3,8,32,512]{3,2,1,0:T(8,128)}, u32[]{:S(2)}) copy-start(f32[3,8,32,512]{3,2,1,0:T(8,128)} %e_in.1) | copy-start | bytes 4718596
  2.7 1.4 %copy-start.1 = (f32[3,8,32,512]{3,2,1,0:T(8,128)S(1)}, f32[3,8,32,512]{3,2,1,0:T(8,128)}, u32[]{:S(2)}) copy-start(f32[3,8,32,512]{3,2,1,0:T(8,128)} %h_in.1) | copy-start | bytes 4718596
  4.1 1.4 %copy-start.2 = (f32[3,8,32,512]{3,2,1,0:T(8,128)S(1)}, f32[3,8,32,512]{3,2,1,0:T(8,128)}, u32[]{:S(2)}) copy-start(f32[3,8,32,512]{3,2,1,0:T(8,128)} %p_in.1) | copy-start | bytes 4718596
  5.5 1.4 %copy-start.3 = (f32[3,8,32,512]{3,2,1,0:T(8,128)S(1)}, f32[3,8,32,512]{3,2,1,0:T(8,128)}, u32[]{:S(2)}) copy-start(f32[3,8,32,512]{3,2,1,0:T(8,128)} %q_in.1) | copy-start | bytes 4718596
  6.9 1.0 %copy-start.4 = (s32[8,32,512]{2,1,0:T(8,128)S(1)}, s32[8,32,512]{2,1,0:T(8,128)}, u32[]{:S(2)}) copy-start(s32[8,32,512]{2,1,0:T(8,128)} %m_in.1) | copy-start | bytes 1572868
  8.0 0.7 copy-start.7
  8.6 0.7 copy-start.8
  9.3 0.7 copy-start.9
  9.9 0.7 copy-start.10
  10.6 33.3 %copy-start.5 = (f32[256,256]{1,0:T(8,128)S(1)}, f32[256,256]{1,0:T(8,128)}, u32[]{:S(2)}) copy-start(f32[256,256]{1,0:T(8,128)} %constant.5.clone.spread) | copy-start | bytes 786436
  10.6 33.3 %copy-start.6 = (f32[16,4096]{1,0:T(8,128)S(1)}, f32[16,4096]{1,0:T(8,128)}, u32[]{:S(2)}) copy-start(f32[16,4096]{1,0:T(8,128)} %constant.4.clone.seeds) | copy-start | bytes 786436

commit v2 on v1

--- a/solution.py
+++ b/solution.py
@@ -21,11 +21,27 @@
 BY = 8
 
 
+def coefficients(nmat, nz, eps, delta, omega, damping):
+    coef = []
+    for m in range(nmat):
+        half = jnp.full((1, nz), damping[m], F32) * (DT / 2.0)
+        denom = 1.0 + half
+        om = jnp.full((1, nz), omega[m], F32)
+        square = om * om * (DT * DT)
+        coef.append((
+            (2.0 - square) / denom,
+            (half - 1.0) / denom,
+            jnp.full((1, nz), delta[m], F32) * square / denom,
+            1.0 / jnp.full((1, nz), eps[m], F32),
+        ))
+    return coef
+
+
 def step_kernel(
     ngx, ngy, nmat,
-    e_in, h_in, p_in, q_in, m_in, eps, delta, omega, damping, flags,
+    e_in, h_in, p_in, q_in, m_in, eps_in, delta_in, omega_in, damping_in, flags_in,
     e_out, h_out, p_out, g_out,
-    E, H, PA, PB, MAT, ystage, ye, yh, gather, G,
+    E, H, PA, PB, MAT, ystage, ye, yh, gather, G, eps, delta, omega, damping, flags,
     in_sem, out_sem, xs_sem, xr_sem, ys_sem, yr_sem, g1s, g1r, g2s, g2r,
 ):
     cx, cy, nz = MAT.shape
@@ -39,6 +55,11 @@
         pltpu.make_async_copy(p_in, PA, in_sem.at[2]),
         pltpu.make_async_copy(q_in, PB, in_sem.at[3]),
         pltpu.make_async_copy(m_in, MAT, in_sem.at[4]),
+        pltpu.make_async_copy(eps_in, eps, in_sem.at[5]),
+        pltpu.make_async_copy(delta_in, delta, in_sem.at[6]),
+        pltpu.make_async_copy(omega_in, omega, in_sem.at[7]),
+        pltpu.make_async_copy(damping_in, damping, in_sem.at[8]),
+        pltpu.make_async_copy(flags_in, flags, in_sem.at[9]),
     ]
     for load in loads:
         load.start()
@@ -69,26 +90,34 @@
 
     def copies(rnd, step):
         if rnd % 2 == 0:
-            xsrc, xdst, ydst = E.at[1:3, 0], E.at[1:3, cx], ye.at[step]
+            field, at_src, at_dst, ydst = E, 0, cx, ye.at[step]
             tx, ty = gx - 1, gy - 1
             sends_x, sends_y = gx > 0, gy > 0
             takes_x, takes_y = gx < ngx - 1, gy < ngy - 1
         else:
-            xsrc, xdst, ydst = H.at[1:3, cx], H.at[1:3, 0], yh.at[step]
+            field, at_src, at_dst, ydst = H, cx, 0, yh.at[step]
             tx, ty = gx + 1, gy + 1
             sends_x, sends_y = gx < ngx - 1, gy < ngy - 1
             takes_x, takes_y = gx > 0, gy > 0
-        xcopy = pltpu.make_async_remote_copy(
-            src_ref=xsrc, dst_ref=xdst, send_sem=xs_sem.at[rnd], recv_sem=xr_sem.at[rnd],
-            device_id=(lax.rem(tx + ngx, ngx), gy), device_id_type=MESH)
+        xcopies = []
+        for i in range(2 * (cy // BY)):
+            c, y = 1 + i % 2, (i // 2) * BY
+            xcopies.append(pltpu.make_async_remote_copy(
+                src_ref=field.at[c, at_src, pl.ds(y, BY)], dst_ref=field.at[c, at_dst, pl.ds(y, BY)],
+                send_sem=xs_sem.at[rnd, i], recv_sem=xr_sem.at[rnd, i],
+                device_id=(lax.rem(tx + ngx, ngx), gy), device_id_type=MESH))
         ycopy = pltpu.make_async_remote_copy(
             src_ref=ystage.at[rnd], dst_ref=ydst, send_sem=ys_sem.at[rnd], recv_sem=yr_sem.at[rnd],
             device_id=(gx, lax.rem(ty + ngy, ngy)), device_id_type=MESH)
-        return xcopy, ycopy, sends_x, sends_y, takes_x, takes_y
-
-    def send_x(rnd, step):
-        xcopy, _, sends_x, _, _, _ = copies(rnd, step)
-        pl.when(sends_x)(xcopy.start)
+        return xcopies, ycopy, sends_x, sends_y, takes_x, takes_y
+
+    def send_x(rnd, step, block):
+        xcopies, _, sends_x, _, _, _ = copies(rnd, step)
+
+        @pl.when(sends_x)
+        def _():
+            for xcopy in xcopies[2 * block : 2 * block + 2]:
+                xcopy.start()
 
     def send_y(rnd, step):
         _, ycopy, _, sends_y, _, _ = copies(rnd, step)
@@ -100,17 +129,25 @@
                     ystage[rnd, i, x : x + 1, :] = H[c, x + 1, cy - 1 : cy, :]
         pl.when(sends_y)(ycopy.start)
 
-    def take_x(rnd, step):
-        xcopy, _, _, _, takes_x, _ = copies(rnd, step)
-        pl.when(takes_x)(xcopy.wait_recv)
+    def take_x(rnd, step, block):
+        xcopies, _, _, _, takes_x, _ = copies(rnd, step)
+
+        @pl.when(takes_x)
+        def _():
+            for xcopy in xcopies[2 * block : 2 * block + 2]:
+                xcopy.wait_recv()
 
     def take_y(rnd, step):
         _, ycopy, _, _, _, takes_y = copies(rnd, step)
         pl.when(takes_y)(ycopy.wait_recv)
 
     def sent_x(rnd, step):
-        xcopy, _, sends_x, _, _, _ = copies(rnd, step)
-        pl.when(sends_x)(xcopy.wait_send)
+        xcopies, _, sends_x, _, _, _ = copies(rnd, step)
+
+        @pl.when(sends_x)
+        def _():
+            for xcopy in xcopies:
+                xcopy.wait_send()
 
     def sent_y(rnd, step):
         _, ycopy, _, sends_y, _, _ = copies(rnd, step)
@@ -131,8 +168,8 @@
     def down_z(v):
         return jnp.where(lane_id == 0, 0.0, pltpu.roll(v, 1, 1))
 
-    def h_plane(step, x):
-        for y in range(0, cy, BY):
+    def h_plane(step, x, blocks):
+        for y in [BY * block for block in blocks]:
             here = pl.ds(y, BY)
             ex, ey, ez = E[0, x, here, :], E[1, x, here, :], E[2, x, here, :]
             if y + BY < cy:
@@ -147,22 +184,9 @@
             H[1, x + 1, here, :] = H[1, x + 1, here, :] - DT * curl_y
             H[2, x + 1, here, :] = H[2, x + 1, here, :] - DT * curl_z
 
-    coef = []
-    for m in range(nmat):
-        half = jnp.full((1, nz), damping[m], F32) * (DT / 2.0)
-        denom = 1.0 + half
-        om = jnp.full((1, nz), omega[m], F32)
-        square = om * om * (DT * DT)
-        coef.append((
-            (2.0 - square) / denom,
-            (half - 1.0) / denom,
-            jnp.full((1, nz), delta[m], F32) * square / denom,
-            1.0 / jnp.full((1, nz), eps[m], F32),
-        ))
-
-    def e_plane(step, x):
+    def e_plane(step, x, coef, blocks):
         now, old = (PA, PB) if step == 0 else (PB, PA)
-        for y in range(0, cy, BY):
+        for y in [BY * block for block in blocks]:
             here = pl.ds(y, BY)
             mat = MAT[x, here, :]
             vox = [jnp.broadcast_to(coef[nmat - 1][i], (BY, nz)) for i in range(4)]
@@ -187,10 +211,9 @@
                 E[i, x, here, :] = e + (DT * curls[i] - (new - p)) * inv
                 old[i, x, here, :] = new
 
-    flag = flags[0, 0].astype(F32)
     surf_lane = lax.broadcasted_iota(jnp.int32, (cy, width), 1)
 
-    def surface(step):
+    def surface(step, flag):
         def body(x, acc):
             base = (gx * cx + x) * 4
             cols = (
@@ -236,9 +259,15 @@
 
     loads[0].wait()
     pl.semaphore_wait(barrier, ngx + ngy - 2)
-    send_x(0, 0)
+    blocks = range(cy // BY)
     send_y(0, 0)
-    loads[1].wait()
+    for block in blocks:
+        send_x(0, 0, block)
+    for load in loads[1:2] + loads[5:]:
+        load.wait()
+
+    coef = coefficients(nmat, nz, eps, delta, omega, damping)
+    flag = flags[0, 0].astype(F32)
 
     for step in range(2):
         down, up = 2 * step, 2 * step + 1
@@ -246,14 +275,15 @@
 
         @pl.loop(0, cx - 1)
         def _(x):
-            h_plane(step, x)
-
-        take_x(down, step)
-        h_plane(step, cx - 1)
-        send_x(up, step)
+            h_plane(step, x, blocks)
+
+        for block in blocks:
+            take_x(down, step, block)
+            h_plane(step, cx - 1, [block])
+            send_x(up, step, block)
         send_y(up, step)
         if step == 0:
-            for load in loads[2:]:
+            for load in loads[2:5]:
                 load.wait()
         else:
             pltpu.make_async_copy(H.at[:, pl.ds(1, cx)], h_out, out_sem.at[0]).start()
@@ -263,15 +293,17 @@
 
         @pl.loop(1, cx)
         def _(x):
-            e_plane(step, x)
-
-        take_x(up, step)
-        e_plane(step, 0)
+            e_plane(step, x, coef, blocks)
+
+        for block in blocks:
+            take_x(up, step, block)
+            e_plane(step, 0, coef, [block])
+            if step == 0:
+                send_x(2, 1, block)
         if step == 0:
-            send_x(2, 1)
             send_y(2, 1)
             sent_x(up, step)
-        surface(step)
+        surface(step, flag)
         gather_first(step)
 
     saves = [
@@ -304,7 +336,7 @@
         wave = 2.0 * math.pi / length
         for angle in (uy, 8.0 * uy, ux, 2.0 * ux):
             rows += [np.cos(wave * angle), np.sin(wave * angle)]
-    return np.stack(rows).astype(np.float32)
+    return np.stack(rows).astype(np.float32).reshape(16, -1, TILE).swapaxes(0, 1).copy()
 
 
 def make_spread():
@@ -320,19 +352,21 @@
 
 def far_kernel(
     nx, ny, g_ref, seeds, spread, e_in, h_in, p_in, far, e_out, h_out, p_out,
-    a_wide, a_low, t_cos, t_sin, s_cos, s_sin, packed, sem,
+    a_wide, a_low, t_cos, t_sin, s_cos, s_sin, packed, e_pass, h_pass, p_pass, sem,
 ):
     pid = pl.program_id(0)
     width = 4 * nx
-    saves = [
-        pltpu.make_async_copy(src, dst, sem.at[i])
-        for i, (src, dst) in enumerate(((e_in, e_out), (h_in, h_out), (p_in, p_out)))
+    tile = pl.num_programs(0) * lax.rem(lax.axis_index("gy"), 2) + pid
+    fields = enumerate(zip((e_in, h_in, p_in), (e_pass, h_pass, p_pass), (e_out, h_out, p_out)))
+    moves = [
+        (pltpu.make_async_copy(src, mid, sem.at[0, i]), pltpu.make_async_copy(mid, dst, sem.at[1, i]))
+        for i, (src, mid, dst) in fields
     ]
 
     @pl.when(pid == 0)
     def _():
-        for save in saves:
-            save.start()
+        for load, _ in moves:
+            load.start()
         for s in range(2):
             a = g_ref[s].T
             high = a.astype(BF16)
@@ -341,6 +375,12 @@
             a_wide[rows, ny : 2 * ny] = high
             a_low[rows, :] = (a - high.astype(F32)).astype(BF16)
 
+    @pl.when(pid == 1)
+    def _():
+        for load, save in moves:
+            load.wait()
+            save.start()
+
     scale = 1.0 / math.sqrt(nx * ny)
     part = 256
     sub = lax.broadcasted_iota(jnp.int32, (8, part), 0)
@@ -351,7 +391,7 @@
 
         def seed(i, lanes):
             row = 8 * f + i
-            return jnp.broadcast_to(seeds[row : row + 1, lanes], (8, part))
+            return jnp.broadcast_to(seeds[tile, row : row + 1, lanes], (8, part))
 
         def times(a, b):
             return (a[0] * b[0] - a[1] * b[1], a[0] * b[1] + a[1] * b[0])
@@ -439,8 +479,33 @@
 
     @pl.when(pid == pl.num_programs(0) - 1)
     def _():
-        for save in saves:
+        for _, save in moves:
             save.wait()
+
+
+def share_kernel(half, far, slots, sem):
+    gx, gy = lax.axis_index("gx"), lax.axis_index("gy")
+    core = lax.rem(gy, 2)
+    other = (gx, gy + 1 - 2 * core)
+    count = half.shape[3]
+    barrier = pltpu.get_barrier_semaphore()
+    pl.semaphore_signal(barrier, inc=1, device_id=other, device_id_type=MESH)
+    pl.semaphore_wait(barrier, 1)
+    sends = []
+    for i in range(4):
+        f, r = i // 2, i % 2
+        send = pltpu.make_async_remote_copy(
+            src_ref=half.at[f, r], dst_ref=slots.at[f, r], send_sem=sem.at[0, i], recv_sem=sem.at[1, i],
+            device_id=other, device_id_type=MESH)
+        send.start()
+        sends.append(send)
+    mine = pl.ds(pl.multiple_of(core * count, count), count)
+    theirs = pl.ds(pl.multiple_of((1 - core) * count, count), count)
+    far[:, :, :, mine] = half[...]
+    for i, send in enumerate(sends):
+        f, r = i // 2, i % 2
+        send.wait()
+        far[f, r, :, theirs] = slots[f, r]
 
 
 def shards(
@@ -452,13 +517,12 @@
     nx, ny = ngx * cx, ngy * cy
     width = 4 * nx
     hbm = pl.BlockSpec(memory_space=pl.ANY)
-    smem = pl.BlockSpec(memory_space=pltpu.SMEM)
     field = jax.ShapeDtypeStruct(e_field.shape, F32)
     dma = pltpu.SemaphoreType.DMA
     e, h, p, g = pl.pallas_call(
         functools.partial(step_kernel, ngx, ngy, eps_table.shape[0]),
         out_shape=(field, field, field, jax.ShapeDtypeStruct((2, ny, width), F32)),
-        in_specs=[hbm] * 5 + [smem] * 5,
+        in_specs=[hbm] * 10,
         out_specs=(hbm,) * 4,
         scratch_shapes=[
             pltpu.VMEM((3, cx + 1, cy, nz), F32),
@@ -471,23 +535,25 @@
             pltpu.VMEM((2, 2, cx, nz), F32),
             pltpu.VMEM((2, ngx, cy, width), F32),
             pltpu.VMEM((2, ny, width), F32),
-            dma((5,)), dma((4,)), dma((4,)), dma((4,)), dma((4,)), dma((4,)),
+            *[pltpu.SMEM(table.shape, F32) for table in (eps_table, delta_table, omega_table, damping_table)],
+            pltpu.SMEM(surface_flags.shape, jnp.int32),
+            dma((10,)), dma((4,)), dma((4, 2 * (cy // BY))), dma((4, 2 * (cy // BY))), dma((4,)), dma((4,)),
             dma((2, ngx)), dma((2, ngx)), dma((2, ngy)), dma((2, ngy)),
         ],
         compiler_params=pltpu.CompilerParams(
-            collective_id=0, has_side_effects=True, vmem_limit_bytes=24 * 1024 * 1024),
+            collective_id=0, has_side_effects=True, vmem_limit_bytes=58 * 1024 * 1024),
     )(e_field, h_field, polar, polar_prev, material,
       eps_table, delta_table, omega_table, damping_table, surface_flags)
 
-    steps = (NDIR // 4) // TILE
+    steps = (NDIR // 4) // TILE // 2
     whole = lambda *shape: pl.BlockSpec(shape, lambda i: (0,) * len(shape))
     far, e, h, p = pl.pallas_call(
         functools.partial(far_kernel, nx, ny),
         grid=(steps,),
-        out_shape=(jax.ShapeDtypeStruct((2, 2, 4, NDIR), F32), field, field, field),
+        out_shape=(jax.ShapeDtypeStruct((2, 2, 4, NDIR // 2), F32), field, field, field),
         in_specs=[
             whole(2, ny, width),
-            pl.BlockSpec((16, TILE), lambda i: (0, i)),
+            whole(2 * steps, 16, TILE),
             whole(256, 256),
             hbm, hbm, hbm,
         ],
@@ -500,10 +566,20 @@
             pltpu.VMEM((2 * width, TILE), F32),
             pltpu.VMEM((2 * width, TILE), F32),
             pltpu.VMEM((4 * (TILE // 128) * 8, 256), F32),
-            dma((3,)),
+            *[pltpu.VMEM(e_field.shape, F32)] * 3,
+            dma((2, 3)),
         ],
-        compiler_params=pltpu.CompilerParams(vmem_limit_bytes=32 * 1024 * 1024),
+        compiler_params=pltpu.CompilerParams(vmem_limit_bytes=56 * 1024 * 1024),
     )(g, jnp.asarray(make_seeds()), jnp.asarray(make_spread()), e, h, p)
+    far = pl.pallas_call(
+        share_kernel,
+        out_shape=jax.ShapeDtypeStruct((2, 2, 4, NDIR), F32),
+        in_specs=[pl.BlockSpec(memory_space=pltpu.VMEM)],
+        out_specs=pl.BlockSpec(memory_space=pltpu.VMEM),
+        scratch_shapes=[pltpu.VMEM((2, 2, 4, NDIR // 2), F32), dma((2, 4))],
+        compiler_params=pltpu.CompilerParams(
+            collective_id=1, has_side_effects=True, vmem_limit_bytes=56 * 1024 * 1024),
+    )(far)
     return e, h, p, far
 
 

time: 67.2 us -> 52.4 us (0.78)
  Pallas kernels: 56.2 us -> 48.6 us
  local copies, waits for them, and re-layouts: 9.29 us -> 2.26 us
    pallas_call x1, Pallas kernels: 22.9 us -> 13.1 us  [shards(): pl.pallas_call(functools.partial(far_kernel, nx, ny), grid=(steps,), out_...]
    unnamed x22 -> x1, local copies, waits for them, and re-layouts: 9.29 us -> 2.26 us
    pallas_call x0 -> x1, Pallas kernels: none -> 4.02 us  [shards(): pl.pallas_call(share_kernel, out_shape=jax.ShapeDtypeStruct((2, 2, 4, NDI...]
    pallas_call x1, Pallas kernels: 33.3 us -> 31.5 us  [shards(): pl.pallas_call(functools.partial(step_kernel, ngx, ngy, eps_table.shape[0...]
where the time goes in v2:
time: 52.4 us; the launch traced here: 52.1 us
  Pallas kernels  48.6 us (93%)
  local copies, waits for them, and re-layouts  2.26 us (4%)
  between operations  1.3 us (2%)
    pallas_call x1, Pallas kernels, shards(): pl.pallas_call(functools.partial(step_kernel, ngx, ngy, eps_table.shape[0...  31.5 us
    pallas_call x1, Pallas kernels, shards(): pl.pallas_call(functools.partial(far_kernel, nx, ny), grid=(steps,), out_...  13.1 us
    pallas_call x1, Pallas kernels, shards(): pl.pallas_call(share_kernel, out_shape=jax.ShapeDtypeStruct((2, 2, 4, NDI...  4.02 us
    unnamed x1, local copies, waits for them, and re-layouts  2.26 us

profile of v2, /device:TPU:0, one launch (start us, length us, event | category | flops | bytes accessed | tf_op | source)
XLA Modules:
  0.0 52.1 jit_solution(12507049940950893098)
XLA Ops:
  1.3 31.5 %shard_map.147 = (f32[3,8,32,512]{3,2,1,0:T(8,128)}, f32[3,8,32,512]{3,2,1,0:T(8,128)}, f32[3,8,32,512]{3,2,1,0:T(8,128)}, f32[2,256,128]{2,1,0:T(8,128)}) custom-call(f32[3,8,32,512]{3,2,1,0:T(8,128)} %e_in.1, f32[3,8,32,512]{3,2,1,0:T(8,128)} %h_in.1, f32[3,8,32,512]{3,2,1,0:T(8,128)} %p_in.1, f32[3,8,32,512]{3,2,1,0:T(8,128)} %q_in.1, ...), custom_call_target="tpu_custom_call" | custom-call | tf_op jit(solution)/shard_map/pallas_call | solution.py:522
  32.8 13.1 %shard_map.148 = (f32[2,2,4,8192]{3,2,1,0:T(4,128)}, f32[3,8,32,512]{3,2,1,0:T(8,128)}, f32[3,8,32,512]{3,2,1,0:T(8,128)}, f32[3,8,32,512]{3,2,1,0:T(8,128)}) custom-call(f32[2,256,128]{2,1,0:T(8,128)} %get-tuple-element.12.g_ref, f32[8,16,512]{2,1,0:T(8,128)} %constant.4.clone.seeds, f32[256,256]{1,0:T(8,128)} %constant.5.clone.spread, ...), custom_call_target="tpu_custom_call" | custom-call | tf_op jit(solution)/shard_map/pallas_call | solution.py:550
  45.8 4.0 %shard_map.149 = f32[2,2,4,16384]{3,2,1,0:T(4,128)} custom-call(f32[2,2,4,8192]{3,2,1,0:T(4,128)} %get-tuple-element.19.half), custom_call_target="tpu_custom_call" | custom-call | tf_op jit(solution)/shard_map/pallas_call | solution.py:574
  49.9 2.3 %copy.18 = f32[2,2,4,16384]{3,2,1,0:T(4,128)} copy(f32[2,2,4,16384]{3,2,1,0:T(4,128)} %shard_map.149) | data formatting | bytes 2097152

commit v3 on v2

--- a/solution.py
+++ b/solution.py
@@ -423,7 +423,7 @@
                     table[pl.ds(pl.multiple_of(at + ny, 16), 16), lanes] = (full - high.astype(F32)).astype(BF16)
                 return times(v, e16) + times(w, e16)
 
-            lax.fori_loop(0, ny // 16, fill, v + w, unroll=4)
+            lax.fori_loop(0, ny // 16, fill, v + w, unroll=16)
 
         for table, result in ((t_cos, s_cos), (t_sin, s_sin)):
             result[...] = jnp.dot(a_wide[...], table[...], preferred_element_type=F32) + jnp.dot(
@@ -443,7 +443,7 @@
                     fresh += [c * w[0], c * w[1], d * w[0], d * w[1]]
                 return times(w, e2) + tuple(t + n for t, n in zip(sums, fresh))
 
-            out = lax.fori_loop(0, nx // 2, add, w0 + (zero,) * 8, unroll=4)
+            out = lax.fori_loop(0, nx // 2, add, w0 + (zero,) * 8, unroll=16)
             sums = out[2:]
             re = [zero] * 4
             im = [zero] * 4

time: 52.4 us -> 48.5 us (0.926)
  Pallas kernels: 48.6 us -> 44.7 us
    pallas_call x1, Pallas kernels: 13.1 us -> 9.21 us  [shards(): pl.pallas_call(functools.partial(far_kernel, nx, ny), grid=(steps,), out_...]
where the time goes in v3:
time: 48.5 us; the launch traced here: 48.3 us
  Pallas kernels  44.7 us (92%)
  local copies, waits for them, and re-layouts  2.26 us (5%)
  between operations  1.3 us (3%)
    pallas_call x1, Pallas kernels, shards(): pl.pallas_call(functools.partial(step_kernel, ngx, ngy, eps_table.shape[0...  31.5 us
    pallas_call x1, Pallas kernels, shards(): pl.pallas_call(functools.partial(far_kernel, nx, ny), grid=(steps,), out_...  9.21 us
    pallas_call x1, Pallas kernels, shards(): pl.pallas_call(share_kernel, out_shape=jax.ShapeDtypeStruct((2, 2, 4, NDI...  4.02 us
    unnamed x1, local copies, waits for them, and re-layouts  2.26 us

profile of v3, /device:TPU:0, one launch (start us, length us, event | category | flops | bytes accessed | tf_op | source)
XLA Modules:
  0.0 48.3 jit_solution(14326738644145518325)
XLA Ops:
  1.3 31.5 %shard_map.147 = (f32[3,8,32,512]{3,2,1,0:T(8,128)}, f32[3,8,32,512]{3,2,1,0:T(8,128)}, f32[3,8,32,512]{3,2,1,0:T(8,128)}, f32[2,256,128]{2,1,0:T(8,128)}) custom-call(f32[3,8,32,512]{3,2,1,0:T(8,128)} %e_in.1, f32[3,8,32,512]{3,2,1,0:T(8,128)} %h_in.1, f32[3,8,32,512]{3,2,1,0:T(8,128)} %p_in.1, f32[3,8,32,512]{3,2,1,0:T(8,128)} %q_in.1, ...), custom_call_target="tpu_custom_call" | custom-call | tf_op jit(solution)/shard_map/pallas_call | solution.py:522
  32.8 9.2 %shard_map.148 = (f32[2,2,4,8192]{3,2,1,0:T(4,128)}, f32[3,8,32,512]{3,2,1,0:T(8,128)}, f32[3,8,32,512]{3,2,1,0:T(8,128)}, f32[3,8,32,512]{3,2,1,0:T(8,128)}) custom-call(f32[2,256,128]{2,1,0:T(8,128)} %get-tuple-element.12.g_ref, f32[8,16,512]{2,1,0:T(8,128)} %constant.4.clone.seeds, f32[256,256]{1,0:T(8,128)} %constant.5.clone.spread, ...), custom_call_target="tpu_custom_call" | custom-call | tf_op jit(solution)/shard_map/pallas_call | solution.py:550
  42.0 4.0 %shard_map.149 = f32[2,2,4,16384]{3,2,1,0:T(4,128)} custom-call(f32[2,2,4,8192]{3,2,1,0:T(4,128)} %get-tuple-element.19.half), custom_call_target="tpu_custom_call" | custom-call | tf_op jit(solution)/shard_map/pallas_call | solution.py:574
  46.0 2.3 %copy.18 = f32[2,2,4,16384]{3,2,1,0:T(4,128)} copy(f32[2,2,4,16384]{3,2,1,0:T(4,128)} %shard_map.149) | data formatting | bytes 2097152
